TPU v7x, 128 devices: a whole 4x4x4 slice. The times are simulated.
128 devices in a mesh: tp: 4 (over z), pool: 32 (over y, x, core).
Axes of the slice: x: 4, y: 4, z: 4, core: 2. Of those that a mesh axis runs over, the one named last changes fastest.
Arguments:
- queries: bfloat16 [512, 4, 8192], P('pool', None, 'tp'), may hold values from -8 to 8
- home_keys: bfloat16 [512, 512, 1024], P('pool', None, 'tp'), may hold values from -6.5 to 6.5
- home_values: bfloat16 [512, 512, 1024], P('pool', None, 'tp'), may hold values from -4 to 4
- new_keys: bfloat16 [512, 4, 1024], P('pool', None, 'tp'), may hold values from -4 to 4
- new_values: bfloat16 [512, 4, 1024], P('pool', None, 'tp'), may hold values from -4 to 4
- home_len: int32 [512], P('pool'), may hold values from 2 to 512
- piece_keys: bfloat16 [512, 256, 1024], P('pool', None, 'tp'), may hold values from -4 to 4
- piece_values: bfloat16 [512, 256, 1024], P('pool', None, 'tp'), may hold values from -4 to 4
- lend_request: int32 [512], P('pool'), may hold values from 0 to 511, as said below
- lend_blocks: int32 [512], P('pool'), may hold values from 1 to 2
- out_weight: bfloat16 [8192, 4096], P('tp'), may hold values from -0.5 to 0.5
Outputs:
- projected: bfloat16 [512, 4, 4096], P('pool', None, 'tp')
Inputs may be any that keep to these rules, and one draw needn't show every extreme that they name: `lend_request`: entries b * 16 to (b + 1) * 16 - 1 are the slots of pool index b. Request r is owned by pool index r // 16. Among the slots of one pool index at most 1 hold requests of the same owner, and some owner has exactly 1 slots on every pool index.
All inputs are finite; a program needn't handle non-finite values.
Results may differ from a plain program's by a relative error of at most 0.0055.
Values may be sent and summed in bfloat16 or wider, within the bound.
A program may use at most 128 MiB of HBM per device.

v0:
```python
import math

import jax
import jax.numpy as jnp
from jax import lax
from jax.sharding import PartitionSpec as P

QH = 64
KVH = 8
HD = 128
BLOCK = 128


MASKED_SCORE = -1e30


def part_summary(score_sets, value_sets, patterns):
    highest = jnp.max(score_sets[0], axis=-1)
    for scores in score_sets[1:]:
        highest = jnp.maximum(highest, jnp.max(scores, axis=-1))
    summed = jnp.zeros(highest.shape, jnp.float32)
    weighted = None
    for scores, values, pattern in zip(score_sets, value_sets, patterns):
        shares = jnp.exp(scores - highest[..., None])
        summed = summed + jnp.sum(shares, axis=-1)
        addend = jnp.einsum(
            pattern, shares.astype(jnp.bfloat16), values, preferred_element_type=jnp.float32
        )
        weighted = addend if weighted is None else weighted + addend
    return (highest + jnp.log(summed), weighted / summed[..., None])


def lent_part(slot_query, piece_keys, piece_values, lend_blocks, kv_dev, per_group, scaling):
    lent_slots = slot_query.shape[0]
    step_count = slot_query.shape[1]
    piece_len = piece_keys.shape[1]
    slot_rows = slot_query.reshape(lent_slots, step_count, kv_dev, per_group, HD)
    keys_piece = piece_keys.reshape(lent_slots, piece_len, kv_dev, HD)
    values_piece = piece_values.reshape(lent_slots, piece_len, kv_dev, HD)
    piece_scores = (
        jnp.einsum("lsgha,ltga->lsght", slot_rows, keys_piece, preferred_element_type=jnp.float32)
        * scaling
    )
    piece_valid = jnp.arange(piece_len, dtype=jnp.int32)[None, :] < (lend_blocks * BLOCK)[:, None]
    piece_scores = jnp.where(piece_valid[:, None, None, None, :], piece_scores, MASKED_SCORE)
    return part_summary([piece_scores], [values_piece], ["lsght,ltga->lsgha"])


def send_back(piece_lse, piece_out, position, pool_size, capacity):
    buffer_len = pool_size * capacity
    out_send = (
        jnp.zeros((buffer_len,) + piece_out.shape[1:], jnp.float32).at[position].set(piece_out)
    )
    lse_send = (
        jnp.full((buffer_len,) + piece_lse.shape[1:], MASKED_SCORE, jnp.float32)
        .at[position]
        .set(piece_lse)
    )
    return (
        lax.all_to_all(
            out_send.reshape((pool_size, capacity) + piece_out.shape[1:]),
            "pool",
            split_axis=0,
            concat_axis=0,
            tiled=True,
        ),
        lax.all_to_all(
            lse_send.reshape((pool_size, capacity) + piece_lse.shape[1:]),
            "pool",
            split_axis=0,
            concat_axis=0,
            tiled=True,
        ),
    )


def per_device(
    queries,
    home_keys,
    home_values,
    new_keys,
    new_values,
    home_len,
    piece_keys,
    piece_values,
    lend_request,
    lend_blocks,
    out_weight,
):
    pool_size = lax.axis_size("pool")
    req_dev = queries.shape[0]
    step_count = queries.shape[1]
    feature_len = queries.shape[2]
    kv_dev = home_keys.shape[2] // HD
    per_group = QH // KVH
    lent_slots = lend_request.shape[0]
    capacity = max(1, 2 * lent_slots // pool_size)
    buffer_len = pool_size * capacity
    scaling = 1.0 / math.sqrt(HD)
    owner_row = lend_request // req_dev
    local_row = lend_request - owner_row * req_dev
    slot_index = jnp.arange(lent_slots, dtype=jnp.int32)
    earlier = (owner_row[None, :] == owner_row[:, None]) & (
        slot_index[None, :] < slot_index[:, None]
    )
    position = owner_row * capacity + jnp.sum(earlier.astype(jnp.int32), axis=1)
    table_send = jnp.full((buffer_len,), -1, jnp.int32).at[position].set(local_row)
    table_recv = lax.all_to_all(
        table_send.reshape(pool_size, capacity), "pool", split_axis=0, concat_axis=0, tiled=True
    ).reshape(buffer_len)
    everyone = lax.all_gather(queries, "pool", axis=0, tiled=True)
    slot_query = jnp.take(everyone, lend_request, axis=0)
    part_lse, part_out = lent_part(
        slot_query, piece_keys, piece_values, lend_blocks, kv_dev, per_group, scaling
    )
    back_out, back_lse = send_back(part_lse, part_out, position, pool_size, capacity)
    home_tokens = home_keys.shape[1]
    query_rows = queries.reshape(req_dev, step_count, kv_dev, per_group, HD)
    keys_home = home_keys.reshape(req_dev, home_tokens, kv_dev, HD)
    values_home = home_values.reshape(req_dev, home_tokens, kv_dev, HD)
    keys_new = new_keys.reshape(req_dev, step_count, kv_dev, HD)
    values_new = new_values.reshape(req_dev, step_count, kv_dev, HD)
    home_scores = (
        jnp.einsum("rsgha,rtga->rghst", query_rows, keys_home, preferred_element_type=jnp.float32)
        * scaling
    )
    home_valid = jnp.arange(home_tokens, dtype=jnp.int32)[None, :] < home_len[:, None]
    home_scores = jnp.where(home_valid[:, None, None, None, :], home_scores, MASKED_SCORE)
    new_scores = (
        jnp.einsum("rsgha,ruga->rghsu", query_rows, keys_new, preferred_element_type=jnp.float32)
        * scaling
    )
    causal = (
        jnp.arange(step_count, dtype=jnp.int32)[None, :]
        <= jnp.arange(step_count, dtype=jnp.int32)[:, None]
    )
    new_scores = jnp.where(causal, new_scores, MASKED_SCORE)
    home_lse, home_out = part_summary(
        [home_scores, new_scores],
        [values_home, values_new],
        ["rghst,rtga->rghsa", "rghsu,ruga->rghsa"],
    )
    got_out = back_out.reshape((buffer_len, step_count, kv_dev, per_group, HD)).transpose(
        0, 2, 3, 1, 4
    )
    got_lse = back_lse.reshape((buffer_len, step_count, kv_dev, per_group)).transpose(0, 2, 3, 1)
    member = table_recv[None, :] == jnp.arange(req_dev, dtype=jnp.int32)[:, None]
    masked = jnp.where(member[:, :, None, None, None], got_lse[None], MASKED_SCORE)
    highest = jnp.maximum(home_lse, jnp.max(masked, axis=1))
    weights = jnp.where(member[:, :, None, None, None], jnp.exp(masked - highest[:, None]), 0.0)
    home_weight = jnp.exp(home_lse - highest)
    numerator = (
        jnp.einsum("rbghs,bghsa->rghsa", weights, got_out, precision=lax.Precision.HIGHEST)
        + home_weight[..., None] * home_out
    )
    denominator = jnp.sum(weights, axis=1) + home_weight
    attention = (
        (numerator / denominator[..., None])
        .transpose(0, 3, 1, 2, 4)
        .reshape(req_dev * step_count, feature_len)
        .astype(jnp.bfloat16)
    )
    partial_out = jnp.dot(attention, out_weight, preferred_element_type=jnp.float32)
    reduced = lax.psum_scatter(partial_out, "tp", scatter_dimension=1, tiled=True)
    return reduced.astype(jnp.bfloat16).reshape(req_dev, step_count, reduced.shape[1])


def solution(mesh):
    placed = (
        P("pool", None, "tp"),
        P("pool", None, "tp"),
        P("pool", None, "tp"),
        P("pool", None, "tp"),
        P("pool", None, "tp"),
        P("pool"),
        P("pool", None, "tp"),
        P("pool", None, "tp"),
        P("pool"),
        P("pool"),
        P("tp", None),
    )
    return jax.shard_map(
        per_device, mesh=mesh, in_specs=placed, out_specs=P("pool", None, "tp"), check_vma=False
    )
```

profile of v0, /device:TPU:0, one launch (start us, length us, event | category | flops | bytes accessed | tf_op | source)
XLA Modules:
  0.0 153.2 jit_solution(11376056260833396537)
XLA Ops:
  6.5 0.7 all-gather.2.cloned.1.call-update
  7.3 0.7 multiply_subtract_fusion
  7.9 0.2 convert_reduce_fusion
  8.1 0.6 scatter_custom_fusion.1
  8.8 0.7 copy.145
  9.4 7.4 %all-to-all-start.1 = ((s32[32,1,1]{2,1,0:T(1,128)}), s32[32,1,1]{2,1,0:T(1,128)S(1)}, u32[]{:S(2)}, u32[]{:S(2)}) async-start(s32[32,1,1]{2,1,0:T(1,128)} %copy.145), calls=%async_computation.1 | async-start | bytes 32768 | tf_op jit(solution)/shard_map/all_to_all | solution.py:108
  16.9 1.1 reshape.169
  18.0 4.0 %reshape.162 = bf16[16,256,2,128]{3,2,1,0:T(2,128)(2,1)} reshape(bf16[16,256,256]{2,1,0:T(8,128)(2,1)} %param.17) | data formatting | bytes 4194304 | tf_op jit(solution)/shard_map/reshape | solution.py:38
  22.0 7.0 %reshape.168 = bf16[16,512,2,128]{3,2,1,0:T(2,128)(2,1)} reshape(bf16[16,512,256]{2,1,0:T(8,128)(2,1)} %param.12) | data formatting | bytes 8388608 | tf_op jit(solution)/shard_map/reshape | solution.py:119
  29.0 5.1 %bitcast_reduce_fusion = (f32[16,2,8,4]{2,3,1,0:T(4,128)S(1)}, f32[16,2,512,4,8]{2,4,3,1,0:T(8,128)}) fusion(pred[16,512]{1,0:T(8,128)(4,1)S(1)} %iota_compare_fusion, bf16[16,4,2,8,128]{4,3,2,1,0:T(8,128)(2,1)S(1)} %reshape.169, bf16[16,512,2,128,1]{3,2,1,0,4:T(2,128)(2,1)} %bitcast.89), kind=kOutput, calls=%fused_computation.9 | convolution fusion | flops 135789568 | bytes 6565888 | tf_op jit(solution)/shard_map/rsgha,rtga->rghst/dot_general | solution.py:124
  34.2 1.3 fusion.74
  35.7 2.3 %fusion.10 = f32[16,2,8,4]{2,3,1,0:T(4,128)S(1)} fusion(f32[16,2,512,4,8]{2,4,3,1,0:T(8,128)} %get-tuple-element.14, f32[16,2,8,4]{2,3,1,0:T(4,128)S(1)} %copy.154, pred[16,512]{1,0:T(8,128)(4,1)S(1)} %iota_compare_fusion), kind=kLoop, calls=%fused_computation.17 | loop fusion | flops 2096128 | bytes 2113536 | tf_op jit(solution)/shard_map/reduce_sum | solution.py:25
  37.9 0.7 copy.156
  38.6 2.1 %reshape.163 = bf16[16,256,2,128]{3,2,1,0:T(2,128)(2,1)} reshape(bf16[16,256,256]{2,1,0:T(8,128)(2,1)S(1)} %copy-done.1) | data formatting | bytes 4194304 | tf_op jit(solution)/shard_map/reshape | solution.py:39
  40.7 7.0 %reshape.171 = bf16[16,512,2,128]{3,2,1,0:T(2,128)(2,1)} reshape(bf16[16,512,256]{2,1,0:T(8,128)(2,1)} %param.13) | data formatting | bytes 8388608 | tf_op jit(solution)/shard_map/reshape | solution.py:120
  47.7 0.6 compare_and_fusion
  48.3 0.7 iota_compare_fusion.1
  49.0 1.1 fusion.57
  50.1 5.0 %fusion = f32[16,2,8,4,128]{4,2,3,1,0:T(8,128)} fusion(bf16[16,512,2,128,1]{3,2,1,0,4:T(2,128)(2,1)} %bitcast.88, f32[16,2,512,4,8]{2,4,3,1,0:T(8,128)} %get-tuple-element.14, f32[16,2,8,4]{2,3,1,0:T(4,128)S(1)} %copy.154, pred[16,512]{1,0:T(8,128)(4,1)S(1)} %iota_compare_fusion), kind=kOutput, calls=%fused_computation.4 | convolution fusion | flops 136314880 | bytes 6828032 | tf_op jit(solution)/shard_map/rghst,rtga->rghsa/dot_general | solution.py:26
  55.1 9.8 %all-gather.2.cloned.1.call-done = bf16[512,4,2048]{2,1,0:T(4,128)(2,1)} async-done(((bf16[16,4,2048]{2,1,0:T(4,128)(2,1)}), bf16[512,4,2048]{2,1,0:T(4,128)(2,1)}) %all-gather.2.cloned.1.call-update) | async-done | bytes 8388624 | tf_op jit(solution)/shard_map/all_gather | solution.py:111
  64.9 4.1 %gather_fusion = bf16[16,4,2048]{2,1,0:T(4,128)(2,1)S(1)} fusion(bf16[512,4,2048]{2,1,0:T(4,128)(2,1)} %all-gather.2.cloned.1.call-done, s32[1024]{0:T(1024)S(1)} %pad_clamp_fusion), kind=kCustom, calls=%fused_computation | custom fusion | bytes 524352 | tf_op jit(solution)/shard_map/jit(_take)/gather | solution.py:112
  69.1 0.9 gather.7
  69.9 1.9 %fusion.73 = (f32[16,4,2,8]{3,1,2,0:T(4,128)S(1)}, f32[16,4,2,8,256]{4,3,1,2,0:T(8,128)S(1)}) fusion(bf16[16,256,2,128,1]{3,2,1,0,4:T(2,128)(2,1)S(1)} %bitcast.90, bf16[16,4,2,8,128]{4,3,2,1,0:T(8,128)(2,1)} %gather.7, pred[16]{0:T(512)(128)(4,1)} %compare_and_fusion, pred[16,256]{1,0:T(8,128)(4,1)} %iota_compare_fusion.1), kind=kOutput, calls=%fused_computation.96 | convolution fusion | flops 68025344 | bytes 3416080 | tf_op jit(solution)/shard_map/lsgha,ltga->lsght/dot_general | solution.py:41
  71.8 0.5 fusion.38
  72.3 0.1 copy-done.5
  72.5 0.7 broadcast_in_dim.121
  73.1 2.3 %scatter_fusion.1 = f32[32,4,2,8]{3,1,2,0:T(4,128)} fusion(f32[32,4,2,8]{3,1,2,0:T(4,128)} %broadcast_in_dim.121, s32[16]{0:T(128)} %copy-done.6, f32[16,4,2,8]{3,1,2,0:T(4,128)S(1)} %bitcast.95), kind=kCustom, calls=%fused_computation.3 | custom fusion | bytes 12352 | tf_op jit(solution)/shard_map/scatter | solution.py:57
  75.4 5.5 %all-to-all-start.2 = ((f32[32,1,4,2,8]{4,2,3,1,0:T(4,128)}), f32[32,1,4,2,8]{4,2,3,1,0:T(4,128)S(1)}, u32[]{:S(2)}, u32[]{:S(2)}) async-start(f32[32,1,4,2,8]{4,2,3,1,0:T(4,128)} %bitcast.9), calls=%async_computation.2 | async-start | bytes 262144 | tf_op jit(solution)/shard_map/all_to_all | solution.py:67
  80.9 2.1 %fusion.25 = f32[16,4,2,8,128]{4,3,1,2,0:T(8,128)S(1)} fusion(bf16[16,256,2,128,1]{3,2,1,0,4:T(2,128)(2,1)} %bitcast.91, f32[16,4,2,8,256]{4,3,1,2,0:T(8,128)S(1)} %get-tuple-element.12, f32[16,4,2,8]{3,1,2,0:T(4,128)} %copy-done.5, f32[16,4,2,8]{3,1,2,0:T(4,128)S(1)} %fusion.38), kind=kOutput, calls=%fused_computation.25 | convolution fusion | flops 67764224 | bytes 3678208 | tf_op jit(solution)/shard_map/lsght,ltga->lsgha/dot_general | solution.py:26
  83.0 0.1 broadcast_in_dim.112
  83.2 0.5 copy-done.7
  83.7 1.1 scatter_fusion
  84.8 1.4 copy.143
  86.2 2.5 %all-to-all-done.2 = f32[32,1,4,2,8]{4,2,3,1,0:T(4,128)S(1)} async-done(((f32[32,1,4,2,8]{4,2,3,1,0:T(4,128)}), f32[32,1,4,2,8]{4,2,3,1,0:T(4,128)S(1)}, u32[]{:S(2)}, u32[]{:S(2)}) %all-to-all-start.2) | async-done | bytes 8224 | tf_op jit(solution)/shard_map/all_to_all | solution.py:67
  88.7 5.0 %all-to-all-start = ((f32[32,1,4,2,8,128]{5,2,4,3,1,0:T(4,128)}), f32[32,1,4,2,8,128]{5,2,4,3,1,0:T(4,128)S(1)}, u32[]{:S(2)}, u32[]{:S(2)}) async-start(f32[32,1,4,2,8,128]{5,2,4,3,1,0:T(4,128)} %copy.143), calls=%async_computation | async-start | bytes 2097152 | tf_op jit(solution)/shard_map/all_to_all | solution.py:60
  93.7 0.2 reduce-scatter.2.cloned.1.call-start
  93.9 0.3 fusion.56
  94.3 0.7 reduce
  95.0 0.3 select_reduce_fusion
  95.4 0.4 fusion.42
  95.9 15.1 %all-to-all-done = f32[32,1,4,2,8,128]{5,2,4,3,1,0:T(4,128)S(1)} async-done(((f32[32,1,4,2,8,128]{5,2,4,3,1,0:T(4,128)}), f32[32,1,4,2,8,128]{5,2,4,3,1,0:T(4,128)S(1)}, u32[]{:S(2)}, u32[]{:S(2)}) %all-to-all-start) | async-done | bytes 1048608 | tf_op jit(solution)/shard_map/all_to_all | solution.py:60
  111.0 1.9 %fusion.28 = bf16[16,4,2,8,128]{4,0,1,3,2:T(8,128)(2,1)S(1)} fusion(f32[32,1,4,2,8,128]{5,2,4,3,1,0:T(4,128)S(1)} %all-to-all-done, f32[16,2,8,4,128]{4,2,3,1,0:T(8,128)S(1)} %copy-done.3, f32[16,2,8,4,128]{4,2,3,1,0:T(8,128)S(1)} %copy-done.12, f32[16,4,2,8]{0,1,3,2:T(4,128)S(1)} %copy.168, f32[16,4,2,8]{0,1,3,2:T(4,128)S(1)} %copy.166, ...), kind=kOutput, calls=%fused_computation.26 | convolution fusion | flops 51216384 | bytes 2384384 | tf_op jit(solution)/shard_map/rbghs,bghsa->rghsa/dot_general | solution.py:153
  113.0 0.2 copy.169
  113.2 0.1 convert_element_type.26
  113.3 9.8 %fusion.75 = f32[64,4096]{1,0:T(8,128)} fusion(bf16[64,2048]{1,0:T(8,128)(2,1)S(1)} %convert_element_type.26, bf16[2048,4096]{1,0:T(8,128)(2,1)} %param.21), kind=kOutput, calls=%fused_computation.98 | convolution fusion | flops 1073741824 | bytes 18087936 | tf_op jit(solution)/shard_map/dot_general | solution.py:163
  123.1 21.6 %reduce-scatter.2.cloned.1.call-done = f32[64,1024]{1,0:T(8,128)} async-done(((f32[64,4096]{1,0:T(8,128)}), f32[64,1024]{1,0:T(8,128)}) %reduce-scatter.2.cloned.1.call-update) | async-done | bytes 262160 | tf_op jit(solution)/shard_map/reduce_scatter | solution.py:164
  144.7 1.0 convert_element_type.27
  145.7 0.7 reshape.173
  (47 shorter events, 0.8 us)
Async XLA Ops:
  6.5 42.5 %copy-start = (bf16[16,4,256]{2,1,0:T(4,128)(2,1)S(1)}, bf16[16,4,256]{2,1,0:T(4,128)(2,1)}, u32[]{:S(2)}) copy-start(bf16[16,4,256]{2,1,0:T(4,128)(2,1)} %param.15) | copy-start | bytes 98308
  6.5 58.4 %all-gather.2.cloned.1.call-start = ((), (), s32[]{:S(2)}) async-start(), calls=%async_computation.4 | async-start | bytes 8650752 | tf_op jit(solution)/shard_map/all_gather | solution.py:111
  8.1 13.9 %copy-start.6 = (s32[16]{0:T(128)}, s32[16]{0:T(128)S(1)}, u32[]{:S(2)}) copy-start(s32[16]{0:T(128)S(1)} %compare_select_fusion) | copy-start | bytes 196
  9.4 66.0 %all-to-all-start.1 = ((s32[32,1,1]{2,1,0:T(1,128)}), s32[32,1,1]{2,1,0:T(1,128)S(1)}, u32[]{:S(2)}, u32[]{:S(2)}) async-start(s32[32,1,1]{2,1,0:T(1,128)} %copy.145), calls=%async_computation.1 | async-start | bytes 32768 | tf_op jit(solution)/shard_map/all_to_all | solution.py:108
  22.0 7.0 %copy-start.8 = (s32[16]{0:T(128)S(1)}, s32[16]{0:T(128)}, u32[]{:S(2)}) copy-start(s32[16]{0:T(128)} %param.16) | copy-start | bytes 196
  29.0 5.2 %copy-start.10 = (bf16[16,4,256]{2,1,0:T(4,128)(2,1)S(1)}, bf16[16,4,256]{2,1,0:T(4,128)(2,1)}, u32[]{:S(2)}) copy-start(bf16[16,4,256]{2,1,0:T(4,128)(2,1)} %param.14) | copy-start | bytes 98308
  34.1 4.6 %copy-start.1 = (bf16[16,256,256]{2,1,0:T(8,128)(2,1)S(1)}, bf16[16,256,256]{2,1,0:T(8,128)(2,1)}, u32[]{:S(2)}) copy-start(bf16[16,256,256]{2,1,0:T(8,128)(2,1)} %param.18) | copy-start | bytes 6291460
  40.7 7.0 %copy-start.9 = (s32[16]{0:T(128)S(1)}, s32[16]{0:T(128)}, u32[]{:S(2)}) copy-start(s32[16]{0:T(128)} %param.19) | copy-start | bytes 196
  40.7 7.6 %copy-start.11 = (s32[16]{0:T(128)S(1)}, s32[16]{0:T(128)}, u32[]{:S(2)}) copy-start(s32[16]{0:T(128)} %param.20) | copy-start | bytes 196
  50.1 19.8 %copy-start.2 = (bf16[16,256,2,128]{3,2,1,0:T(2,128)(2,1)S(1)}, bf16[16,256,2,128]{3,2,1,0:T(2,128)(2,1)}, u32[]{:S(2)}) copy-start(bf16[16,256,2,128]{3,2,1,0:T(2,128)(2,1)} %reshape.162) | copy-start | bytes 6291460
  71.8 0.6 copy-start.5
  75.4 13.3 %all-to-all-start.2 = ((f32[32,1,4,2,8]{4,2,3,1,0:T(4,128)}), f32[32,1,4,2,8]{4,2,3,1,0:T(4,128)S(1)}, u32[]{:S(2)}, u32[]{:S(2)}) async-start(f32[32,1,4,2,8]{4,2,3,1,0:T(4,128)} %bitcast.9), calls=%async_computation.2 | async-start | bytes 262144 | tf_op jit(solution)/shard_map/all_to_all | solution.py:67
  83.0 0.7 copy-start.7
  84.7 10.6 %copy-start.4 = (f32[16,2,8,4]{0,2,1,3:T(8,128)S(1)}, f32[16,2,8,4]{0,2,1,3:T(8,128)}, u32[]{:S(2)}) copy-start(f32[16,2,8,4]{0,2,1,3:T(8,128)} %copy.156) | copy-start | bytes 12292
  86.2 24.9 %copy-start.3 = (f32[16,2,8,4,128]{4,2,3,1,0:T(8,128)S(1)}, f32[16,2,8,4,128]{4,2,3,1,0:T(8,128)}, u32[]{:S(2)}) copy-start(f32[16,2,8,4,128]{4,2,3,1,0:T(8,128)} %fusion.57) | copy-start | bytes 1572868
  86.2 24.9 %copy-start.12 = (f32[16,2,8,4,128]{4,2,3,1,0:T(8,128)S(1)}, f32[16,2,8,4,128]{4,2,3,1,0:T(8,128)}, u32[]{:S(2)}) copy-start(f32[16,2,8,4,128]{4,2,3,1,0:T(8,128)} %fusion) | copy-start | bytes 1572868
  88.7 22.4 %all-to-all-start = ((f32[32,1,4,2,8,128]{5,2,4,3,1,0:T(4,128)}), f32[32,1,4,2,8,128]{5,2,4,3,1,0:T(4,128)S(1)}, u32[]{:S(2)}, u32[]{:S(2)}) async-start(f32[32,1,4,2,8,128]{5,2,4,3,1,0:T(4,128)} %copy.143), calls=%async_computation | async-start | bytes 2097152 | tf_op jit(solution)/shard_map/all_to_all | solution.py:60
  93.7 51.0 %reduce-scatter.2.cloned.1.call-start = ((), (), s32[]{:S(2)}) async-start(), calls=%async_computation.5 | async-start | bytes 1310720 | tf_op jit(solution)/shard_map/reduce_scatter | solution.py:164
Sparse Core Ops, SparseCore 0:
  9.6 55.2 all-gather.1
  123.2 21.4 reduce-scatter.1
where the time goes:
time: 154 us; the launch traced here: 153 us
  waiting for transfers between devices  49.8 us (32%)
  local copies, waits for them, and re-layouts  36 us (23%)
  matrix products  28.1 us (18%)
  starting transfers between devices  18.1 us (12%)
  between operations  13.6 us (9%)
  other arithmetic  7.54 us (5%)
    reduce_scatter x1, waiting for transfers between devices, per_device(): lax.psum_scatter(partial_out, 'tp', scatter_dimension=1, tiled=True)  21.6 us
    all_to_all x1, waiting for transfers between devices, send_back(): lax.all_to_all(out_send.reshape((pool_size, capacity) + piece_out.shape[1...  15.1 us
    all_gather x1, waiting for transfers between devices, per_device(): everyone = lax.all_gather(queries, 'pool', axis=0, tiled=True)  9.85 us
    dot_general x1, matrix products, per_device(): jnp.dot(attention, out_weight, preferred_element_type=jnp.float32)  9.78 us
    dot_general x3, matrix products, part_summary(): jnp.einsum(pattern, shares.astype(jnp.bfloat16), values, preferred_elemen...  8.16 us
    all_to_all x1, starting transfers between devices, per_device(): lax.all_to_all(table_send.reshape(pool_size, capacity), 'pool', split_axi...  7.4 us
    reshape x1, local copies, waits for them, and re-layouts, per_device(): values_home = home_values.reshape(req_dev, home_tokens, kv_dev, HD)  7 us
    reshape x1, local copies, waits for them, and re-layouts, per_device(): keys_home = home_keys.reshape(req_dev, home_tokens, kv_dev, HD)  6.96 us
  transfers between devices with their start and end apart: 5, of which 4 were waited for; matrix products, arithmetic and copies ran while one was open for 37% of the time, Pallas kernels for 0%

commit v1 on v0

v1 whole, which is shorter than its diff:
```python
import functools
import math

import jax
import jax.numpy as jnp
from jax import lax
from jax.experimental import pallas as pl
from jax.experimental.pallas import tpu as pltpu
from jax.sharding import PartitionSpec as P

QH = 64
KVH = 8
HD = 128
BLOCK = 128
MASKED = -1e30
MESH = pl.DeviceIdType.MESH
F32 = jnp.float32
BF16 = jnp.bfloat16
COEF = math.log2(math.e) / math.sqrt(HD)


def nt(a, b):
    return lax.dot_general(a, b, (((1,), (1,)), ((), ())), preferred_element_type=F32)


def nn(a, b):
    return lax.dot_general(a, b, (((1,), (0,)), ((), ())), preferred_element_type=F32)


def iota(shape, dim):
    return lax.broadcasted_iota(jnp.int32, shape, dim)


def attend(q, keys, values, valid_len, new_scores, new_values):
    half = q.shape[0] // 2
    zero = jnp.zeros((half, HD), BF16)
    wide = jnp.concatenate(
        [
            jnp.concatenate([q[:half], zero], axis=1),
            jnp.concatenate([zero, q[half:]], axis=1),
        ],
        axis=0,
    )
    scores = nt(wide, keys)
    scores = jnp.where(iota(scores.shape, 1) < valid_len, scores, MASKED)
    top = jnp.max(scores, axis=1, keepdims=True)
    top = jnp.maximum(top, jnp.max(new_scores, axis=1, keepdims=True))
    shares = jnp.exp2((scores - top) * COEF)
    summed = jnp.sum(shares, axis=1, keepdims=True)
    both = nn(shares.astype(BF16), values)
    out = jnp.concatenate([both[:half, :HD], both[half:, HD:]], axis=0)
    new_shares = jnp.exp2((new_scores - top) * COEF)
    summed = summed + jnp.sum(new_shares, axis=1, keepdims=True)
    out = out + nn(new_shares.astype(BF16), new_values)
    return (out / summed).astype(BF16), top * COEF + jnp.log2(summed)


def head_shares(q, keys, valid_len):
    scores = nt(q, keys)
    scores = jnp.where(iota(scores.shape, 1) < valid_len, scores, MASKED)
    top = jnp.max(scores, axis=1, keepdims=True)
    shares = jnp.exp2((scores - top) * COEF)
    summed = jnp.sum(shares, axis=1, keepdims=True)
    return shares.astype(BF16), summed, top * COEF + jnp.log2(summed)


def kernel(
    n, t,
    hlen_h, lreq_h, lblk_h, q_h, nk_h, nv_h, hk_h, hv_h, pk_h, pv_h, w_h,
    out_ref,
    hlen, lreq, lblk, q_v, nk_v, nv_v, hk_v, hv_v, pk_v, pv_v, w_v,
    sn_v, tab_s, tab_r, inv_v, inv_s,
    qs0_v, qs1_v, qr0_v, qr1_v, res_v, sh_v, rs0_v, rs1_v, rr0_v, rr1_v, ls_v, lr_v,
    ho_v, hl_c, pl_c, e_v, t_v, a0_v, a1_v, acc_v, ps_v, pr_v,
    in_sem, home_sem, w_sem, send_sem, recv_sem, rsend_sem, rrecv_sem,
):
    me = lax.axis_index("pool")
    tp = lax.axis_index("tp")
    reqs, rows, _ = q_v.shape
    slots = pk_v.shape[0]
    steps = 4
    home_chunks = home_sem.shape[1]
    per_chunk = reqs // home_chunks
    cols = w_v.shape[2]
    part_rows = rows // 2
    deep = a0_v.shape[1]
    qs, qr = (qs0_v, qs1_v), (qr0_v, qr1_v)
    rs, rr = (rs0_v, rs1_v), (rr0_v, rr1_v)

    def pool_peer(d):
        return jnp.where(me + d >= n, me + d - n, me + d)

    def tp_peer(d):
        return lax.rem(tp + d, t)

    barrier = pltpu.get_barrier_semaphore()

    for d in range(1, n):
        pl.semaphore_signal(
            barrier, inc=1, device_id={"pool": pool_peer(d)}, device_id_type=MESH
        )
    for d in range(1, t):
        pl.semaphore_signal(
            barrier, inc=1, device_id={"tp": tp_peer(d)}, device_id_type=MESH
        )

    small = [
        pltpu.make_async_copy(src, dst, in_sem.at[i])
        for i, (src, dst) in enumerate(
            [
                (q_h, q_v), (nk_h, nk_v), (nv_h, nv_v), (pk_h, pk_v), (pv_h, pv_v),
                (lreq_h, lreq), (hlen_h, hlen), (lblk_h, lblk),
            ]
        )
    ]
    for i in (5, 6, 7, 0, 1, 2):
        small[i].start()
    home = []
    for c in range(home_chunks):
        part = pl.ds(c * per_chunk, per_chunk)
        home.append(
            [
                pltpu.make_async_copy(hk_h.at[part], hk_v.at[part], home_sem.at[0, c]),
                pltpu.make_async_copy(hv_h.at[part], hv_v.at[part], home_sem.at[1, c]),
            ]
        )
    order = [2, 1, 3, 0]
    weights = []
    for i, d in enumerate(order):
        column = pl.multiple_of(tp_peer(d) * cols, cols)
        weights.append(
            pltpu.make_async_copy(w_h.at[:, pl.ds(column, cols)], w_v.at[i], w_sem.at[i])
        )

    for i in (5, 6, 7):
        small[i].wait()
    owner_id = iota((n, 128), 0)
    wanted = jnp.full((n, 128), -1, jnp.int32)
    slot_of = jnp.zeros((n, 128), jnp.int32)
    for l in range(slots):
        request = lreq[l]
        owner = request // reqs
        hit = owner_id == owner
        wanted = jnp.where(hit, request - owner * reqs, wanted)
        slot_of = jnp.where(hit, l, slot_of)
    tab_s[...] = wanted.reshape(n, 1, 128)
    inv_v[...] = slot_of.reshape(n, 1, 128)

    def remote(phase, src, dst, d):
        return pltpu.make_async_remote_copy(
            src_ref=src,
            dst_ref=dst,
            send_sem=send_sem.at[phase],
            recv_sem=recv_sem.at[phase],
            device_id={"pool": pool_peer(d)},
            device_id_type=MESH,
        )

    def all_of(phase, buffer):
        part = buffer.at[pl.ds(0, n - 1)]
        return remote(phase, part, part, 1)

    pl.semaphore_wait(barrier, n - 1 + t - 1)

    for d in range(1, n):
        remote(0, tab_s.at[pool_peer(d)], tab_r.at[me], d).start()
    tab_r[me] = tab_s[me]
    for c in range(home_chunks):
        home[c][0].start()
        home[c][1].start()
    small[3].start()
    small[4].start()

    for copy in small[:3]:
        copy.wait()
    sn_v[...] = nt(q_v[...].reshape(reqs * rows, HD), nk_v[...]).reshape(reqs, rows, HD)
    hl_c[...] = jnp.zeros(hl_c.shape, F32)
    pl_c[...] = jnp.zeros(pl_c.shape, F32)
    lane = iota((rows, 128), 1)
    row = iota((rows, 128), 0)

    def home_request(r):
        low = r * (2 * steps) + (row // (rows // 2)) * steps
        seen = (lane >= low) & (lane <= low + row % steps)
        new_scores = jnp.where(seen, sn_v[r], MASKED)
        out, lse = attend(q_v[r], hk_v[r], hv_v[r], hlen[r], new_scores, nv_v[...])
        ho_v[r] = out
        return lse

    def home_pair(i, carry):
        lse0 = home_request(2 * i)
        lse1 = home_request(2 * i + 1)
        hl_c[0:rows] = jnp.where(
            lane == 2 * i, lse0, jnp.where(lane == 2 * i + 1, lse1, hl_c[0:rows])
        )
        return carry

    def home_part(c):
        home[c][0].wait()
        home[c][1].wait()
        lax.fori_loop(c * per_chunk // 2, (c + 1) * per_chunk // 2, home_pair, 0)

    home_part(0)

    all_of(0, tab_r).wait_recv()

    picks = [jnp.maximum(tab_r[pool_peer(d), 0, 0], 0) for d in range(1, n)]
    mine = jnp.maximum(tab_r[me, 0, 0], 0)
    halves = [slice(0, part_rows), slice(part_rows, rows)]

    def send_query(k, d):
        peer = pool_peer(d)
        qs[k][peer] = q_v[picks[d - 1], halves[k]]
        remote(1 + k, qs[k].at[peer], qr[k].at[me], d).start()

    for k in range(2):
        qr[k][me] = q_v[mine, halves[k]]
    for d in range(1, n):
        send_query(0, d)
    for copy in weights:
        copy.start()

    home[1][0].wait()
    home[1][1].wait()
    for i in range(per_chunk // 2):
        for d in range(1 + i * 16, min(n, 17 + i * 16)):
            send_query(1, d)
        home_pair(per_chunk // 2 + i, 0)
    for d in range(n):
        inv_s[d] = inv_v[pool_peer(d), 0, 0]

    small[3].wait()
    small[4].wait()
    part_lane = iota((part_rows, 128), 1)

    def send_result(k, d):
        peer = pool_peer(d)
        rs[k][peer] = res_v[inv_s[d], halves[k]]
        remote(4 + k, rs[k].at[peer], rr[k].at[me], d).start()

    def send_lse(d):
        remote(3, ls_v.at[pool_peer(d)], lr_v.at[me], d).start()

    for k in range(2):
        all_of(1 + k, qr[k]).wait_recv()
        width = slice(k * HD, k * HD + HD)
        total = jnp.zeros((part_rows, 128), F32)
        sums = []
        for l in range(slots):
            owner = lreq[l] // reqs
            shares, summed, lse = head_shares(qr[k][owner], pk_v[l, :, width], lblk[l] * BLOCK)
            sh_v[l] = shares
            sums.append(summed)
            total = jnp.where(part_lane == owner, lse, total)
            if k == 1:
                for d in (2 * l, 2 * l + 1):
                    if d > 0:
                        send_result(0, d)
        pl_c[halves[k]] = total
        if k == 1:
            ls_v[...] = pl_c[...].T[0:n].reshape(n, 1, 128)
            lr_v[me] = ls_v[me]
        for l in range(slots):
            out = nn(sh_v[l], pv_v[l, :, width])
            res_v[l, halves[k]] = (out / sums[l]).astype(BF16)
            if k == 1:
                for d in (2 * l, 2 * l + 1):
                    if d > 0:
                        send_lse(d)
        rr[k][me] = res_v[inv_s[0], halves[k]]
    for d in range(1, n):
        send_result(1, d)

    for c in range(2, home_chunks):
        home_part(c)

    eight = iota((8, 128), 1) // 16 == iota((8, 128), 0)
    local = tab_r[...].reshape(n, 128)
    parts = n + reqs
    seg = jnp.concatenate([local, iota((reqs, 128), 0)], axis=0)
    seg_lane = jnp.concatenate(
        [
            jnp.sum(jnp.where(eight, seg[c * 8 : c * 8 + 8], 0), axis=0, keepdims=True)
            for c in range(parts // 8)
        ],
        axis=1,
    )
    block = (16, parts * 16)
    b_row, b_col = iota(block, 0), iota(block, 1)
    head_step = b_col % 16 - b_row % steps
    owner_row = seg_lane - b_row // steps
    for i in range(16):
        same = (head_step == i // 4 * steps) & (owner_row == i % 4 * 4)
        e_v[i] = jnp.where(same, 1.0, 0.0).astype(BF16)
    t_row = iota(t_v.shape, 0)
    t_col = iota(t_v.shape, 1)
    t_v[...] = jnp.where(
        t_row == (t_col // 128) * 16 + t_col % 16, 1.0, 0.0
    ).astype(BF16)

    all_of(3, lr_v).wait_recv()
    lse = jnp.concatenate([lr_v[...].reshape(n, 128), hl_c[...].T[0:reqs]], axis=0)
    big = lse
    for r in range(reqs):
        hit = seg == r
        big = jnp.where(hit, jnp.max(jnp.where(hit, lse, MASKED), axis=0, keepdims=True), big)
    share = jnp.where(seg >= 0, jnp.exp2(lse - big), 0.0)
    total = jnp.ones_like(share)
    for r in range(reqs):
        hit = seg == r
        total = jnp.where(
            hit, jnp.sum(jnp.where(hit, share, 0.0), axis=0, keepdims=True), total
        )
    spread = nn((share / total).astype(BF16), t_v[...])

    def merge(k, a_v):
        all_of(4 + k, rr[k]).wait_recv()
        for g in range(part_rows // 16):
            wide = (k * (part_rows // 16) + g) * 128
            along = jnp.concatenate(
                [
                    jnp.sum(
                        jnp.where(
                            eight, spread[c * 8 : c * 8 + 8, wide : wide + 128], 0.0
                        ),
                        axis=0,
                        keepdims=True,
                    )
                    for c in range(parts // 8)
                ],
                axis=1,
            )
            along = jnp.broadcast_to(along, block).astype(BF16)
            left = (e_v[...] * along[None]).reshape(256, parts * 16)
            group = slice(g * 16, g * 16 + 16)
            own = slice(k * part_rows + g * 16, k * part_rows + g * 16 + 16)
            right = jnp.concatenate(
                [rr[k][:, group].reshape(n * 16, HD), ho_v[:, own].reshape(reqs * 16, HD)],
                axis=0,
            )
            merged = nn(left, right).astype(BF16)
            for h in range(4):
                head = g * 4 + h
                a_v[:, head * HD : head * HD + HD] = merged[h * rows : h * rows + rows]

    merge(0, a0_v)
    for i in range(t):
        weights[i].wait()
        acc_v[i] = nn(a0_v[...], w_v[i, 0:deep])
    merge(1, a1_v)

    def projected(i):
        return acc_v[i] + nn(a1_v[...], w_v[i, deep : 2 * deep])

    half = cols // 2

    def to_neighbour(i, src, side):
        return pltpu.make_async_remote_copy(
            src_ref=src,
            dst_ref=pr_v.at[i],
            send_sem=rsend_sem.at[i],
            recv_sem=rrecv_sem.at[i],
            device_id={"tp": tp_peer(side)},
            device_id_type=MESH,
        )

    up, down = 1, t - 1
    hops = [
        to_neighbour(i, ps_v.at[i], side)
        for i, side in enumerate([up, down, up, down, up, down])
    ]
    for i in range(2):
        at = slice(i * half, i * half + half)
        value = acc_v[0, :, at] + nn(a1_v[...], w_v[0, deep : 2 * deep, at])
        ps_v[i] = value.astype(BF16)
        hops[i].start()
    above = projected(1)
    ps_v[2] = above[:, half:].astype(BF16)
    hops[2].start()
    acc_v[1, :, :half] = above[:, :half]
    below = projected(2)
    ps_v[3] = below[:, :half].astype(BF16)
    hops[3].start()
    hops[0].wait_recv()
    ps_v[4] = (acc_v[1, :, :half] + pr_v[0].astype(F32)).astype(BF16)
    hops[4].start()
    hops[1].wait_recv()
    ps_v[5] = (below[:, half:] + pr_v[1].astype(F32)).astype(BF16)
    hops[5].start()
    acc_v[3] = projected(3)
    for i in range(2, 6):
        hops[i].wait_recv()
    from_below = jnp.concatenate([pr_v[4], pr_v[2]], axis=1).astype(F32)
    from_above = jnp.concatenate([pr_v[3], pr_v[5]], axis=1).astype(F32)
    result = acc_v[3] + from_below + from_above

    first = iota((8, 8, HD), 1) < 4
    for g in range(2):
        even, odd = [], []
        for k in range(2):
            c = (g * 2 + k) * 2 * HD
            left = result[:, c : c + HD].reshape(8, 8, HD)
            right = result[:, c + HD : c + 2 * HD].reshape(8, 8, HD)
            even.append(jnp.where(first, left, pltpu.roll(right, 4, 1)))
            odd.append(jnp.where(first, pltpu.roll(left, 4, 1), right))
        for k, both in enumerate([even, odd]):
            out_ref[:, k, g * 16 : g * 16 + 16] = jnp.concatenate(both, axis=1).astype(BF16)

    all_of(0, tab_s).wait_send()
    for k in range(2):
        all_of(1 + k, qs[k]).wait_send()
        all_of(4 + k, rs[k]).wait_send()
    all_of(3, ls_v).wait_send()
    for hop in hops:
        hop.wait_send()


def per_device(
    queries, home_keys, home_values, new_keys, new_values, home_len,
    piece_keys, piece_values, lend_request, lend_blocks, out_weight,
):
    n = lax.axis_size("pool")
    t = lax.axis_size("tp")
    reqs, steps, features = queries.shape
    heads = features // HD
    kv = new_keys.shape[2] // HD
    rows = heads * steps
    slots, piece = piece_keys.shape[:2]
    cols = out_weight.shape[1] // t

    def head_rows(x):
        count = x.shape[2] // HD
        return x.reshape(reqs, steps, count, HD).transpose(0, 2, 1, 3)

    q = head_rows(queries).reshape(reqs, rows, HD)
    nk = head_rows(new_keys).reshape(reqs * kv * steps, HD)
    nv = head_rows(new_values).reshape(reqs * kv * steps, HD)
    hbm = pl.BlockSpec(memory_space=pl.ANY)
    chunks = 4
    vmem = pltpu.VMEM
    out = pl.pallas_call(
        functools.partial(kernel, n, t),
        out_shape=vmem((reqs // 2, 2, cols // HD * steps, HD), BF16),
        in_specs=[hbm] * 11,
        out_specs=pl.BlockSpec(memory_space=pltpu.VMEM),
        scratch_shapes=[
            *[pltpu.SMEM((reqs,), jnp.int32)] * 3,
            vmem(q.shape, BF16),
            vmem(nk.shape, BF16),
            vmem(nv.shape, BF16),
            vmem(home_keys.shape, BF16),
            vmem(home_values.shape, BF16),
            vmem(piece_keys.shape, BF16),
            vmem(piece_values.shape, BF16),
            vmem((t, features, cols), BF16),
            vmem((reqs, rows, 128), F32),
            vmem((n, 1, 128), jnp.int32),
            vmem((n, 1, 128), jnp.int32),
            vmem((n, 1, 128), jnp.int32),
            pltpu.SMEM((n,), jnp.int32),
            *[vmem((n, rows // 2, HD), BF16)] * 4,
            vmem((slots, rows, HD), BF16),
            vmem((slots, rows // 2, piece), BF16),
            *[vmem((n, rows // 2, HD), BF16)] * 4,
            *[vmem((n, 1, 128), F32)] * 2,
            vmem((reqs, rows, HD), BF16),
            *[vmem((128, 128), F32)] * 2,
            vmem((16, 16, (n + reqs) * 16), BF16),
            vmem((128, (rows // 16) * 128), BF16),
            *[vmem((reqs * steps, features // 2), BF16)] * 2,
            vmem((t, reqs * steps, cols), F32),
            vmem((6, reqs * steps, cols // 2), BF16),
            vmem((6, reqs * steps, cols // 2), BF16),
            pltpu.SemaphoreType.DMA((8,)),
            pltpu.SemaphoreType.DMA((2, chunks)),
            pltpu.SemaphoreType.DMA((t,)),
            pltpu.SemaphoreType.DMA((6,)),
            pltpu.SemaphoreType.DMA((6,)),
            pltpu.SemaphoreType.DMA((6,)),
            pltpu.SemaphoreType.DMA((6,)),
        ],
        compiler_params=pltpu.CompilerParams(
            collective_id=0, has_side_effects=True, vmem_limit_bytes=56 * 1024 * 1024
        ),
        name="lent_attention",
    )(
        home_len, lend_request, lend_blocks, q, nk, nv,
        home_keys, home_values, piece_keys, piece_values, out_weight,
    )
    out = out.reshape(reqs, cols // HD, steps, HD).transpose(0, 2, 1, 3)
    return out.reshape(reqs, steps, cols)


def solution(mesh):
    placed = (
        P("pool", None, "tp"),
        P("pool", None, "tp"),
        P("pool", None, "tp"),
        P("pool", None, "tp"),
        P("pool", None, "tp"),
        P("pool"),
        P("pool", None, "tp"),
        P("pool", None, "tp"),
        P("pool"),
        P("pool"),
        P("tp", None),
    )
    return jax.shard_map(
        per_device, mesh=mesh, in_specs=placed, out_specs=P("pool", None, "tp"), check_vma=False
    )
```

time: 154 us -> 39.2 us (0.25)
  waiting for transfers between devices: 49.8 us -> 0 us
  Pallas kernels: 0 us -> 38.4 us
  local copies, waits for them, and re-layouts: 36 us -> 0.66 us
  matrix products: 28.1 us -> 0 us
  starting transfers between devices: 18.1 us -> 0 us
  between operations: 13.6 us -> 0.01 us
  other arithmetic: 7.54 us -> 0 us
    pallas_call x0 -> x1, Pallas kernels: none -> 38.4 us  [per_device(): pl.pallas_call(functools.partial(kernel, n, t), out_shape=vmem((reqs // 2...]
    dot_general x8 -> x0, matrix products: 28.1 us -> none  [the longest x1 9.78 us: per_device(): jnp.dot(attention, out_weight, preferred_element_type=jnp.float32)]
    reshape x7 -> x0, local copies, waits for them, and re-layouts: 23.3 us -> none  [the longest x1 7 us: per_device(): values_home = home_values.reshape(req_dev, home_tokens, kv_dev, HD)]
    reduce_scatter x1 -> x0, waiting for transfers between devices: 21.6 us -> none  [per_device(): lax.psum_scatter(partial_out, 'tp', scatter_dimension=1, tiled=True)]
    all_to_all x3 -> x0, starting transfers between devices: 17.9 us -> none  [the longest x1 7.4 us: per_device(): lax.all_to_all(table_send.reshape(pool_size, capacity), 'pool', split_axi...]
    all_to_all x3 -> x0, waiting for transfers between devices: 17.6 us -> none  [the longest x1 15.1 us: send_back(): lax.all_to_all(out_send.reshape((pool_size, capacity) + piece_out.shape[1...]
    all_gather x1 -> x0, waiting for transfers between devices: 9.85 us -> none  [per_device(): everyone = lax.all_gather(queries, 'pool', axis=0, tiled=True)]
    gather x2 -> x0, local copies, waits for them, and re-layouts: 5.01 us -> none  [per_device(): slot_query = jnp.take(everyone, lend_request, axis=0)]
  transfers between devices with their start and end apart: 5 -> 0, of which waited for: 4 -> 0; matrix products, arithmetic and copies ran while one was open for 37% -> 0% of each run, Pallas kernels for 0% -> 0%
where the time goes in v1:
time: 39.2 us; the launch traced here: 39.1 us
  Pallas kernels  38.4 us (98%)
  local copies, waits for them, and re-layouts  0.66 us (2%)
    pallas_call x1, Pallas kernels, per_device(): pl.pallas_call(functools.partial(kernel, n, t), out_shape=vmem((reqs // 2...  38.4 us

profile of v1, /device:TPU:0, one launch (start us, length us, event | category | flops | bytes accessed | tf_op | source)
XLA Modules:
  0.0 39.1 jit_solution(1798870226666369095)
XLA Ops:
  0.0 38.4 %lent_attention.1 = bf16[8,2,32,128]{3,2,1,0:T(8,128)(2,1)S(1)} custom-call(s32[16]{0:T(128)} %hlen_h.1, s32[16]{0:T(128)} %lreq_h.1, s32[16]{0:T(128)} %lblk_h.1, bf16[16,64,128]{2,1,0:T(8,128)(2,1)} %bitcast.21, bf16[128,128]{1,0:T(8,128)(2,1)} %bitcast.22, bf16[128,128]{1,0:T(8,128)(2,1)} %bitcast.23, bf16[16,512,256]{2,1,0:T(8,128)(2,1)} %hk_h.1, ...), custom_call_target="tpu_custom_call" | custom-call | tf_op jit(solution)/shard_map/lent_attention/pallas_call | solution.py:441
  38.4 0.7 %copy.17 = bf16[16,4,1024]{2,1,0:T(4,128)(2,1)} copy(bf16[16,4,1024]{2,1,0:T(4,128)(2,1)S(1)} %bitcast.20) | data formatting | bytes 262144

commit v2 on v1

--- a/solution.py
+++ b/solution.py
@@ -31,28 +31,16 @@
     return lax.broadcasted_iota(jnp.int32, shape, dim)
 
 
-def attend(q, keys, values, valid_len, new_scores, new_values):
+def wide_query(q):
     half = q.shape[0] // 2
     zero = jnp.zeros((half, HD), BF16)
-    wide = jnp.concatenate(
+    return jnp.concatenate(
         [
             jnp.concatenate([q[:half], zero], axis=1),
             jnp.concatenate([zero, q[half:]], axis=1),
         ],
         axis=0,
     )
-    scores = nt(wide, keys)
-    scores = jnp.where(iota(scores.shape, 1) < valid_len, scores, MASKED)
-    top = jnp.max(scores, axis=1, keepdims=True)
-    top = jnp.maximum(top, jnp.max(new_scores, axis=1, keepdims=True))
-    shares = jnp.exp2((scores - top) * COEF)
-    summed = jnp.sum(shares, axis=1, keepdims=True)
-    both = nn(shares.astype(BF16), values)
-    out = jnp.concatenate([both[:half, :HD], both[half:, HD:]], axis=0)
-    new_shares = jnp.exp2((new_scores - top) * COEF)
-    summed = summed + jnp.sum(new_shares, axis=1, keepdims=True)
-    out = out + nn(new_shares.astype(BF16), new_values)
-    return (out / summed).astype(BF16), top * COEF + jnp.log2(summed)
 
 
 def head_shares(q, keys, valid_len):
@@ -71,7 +59,7 @@
     hlen, lreq, lblk, q_v, nk_v, nv_v, hk_v, hv_v, pk_v, pv_v, w_v,
     sn_v, tab_s, tab_r, inv_v, inv_s,
     qs0_v, qs1_v, qr0_v, qr1_v, res_v, sh_v, rs0_v, rs1_v, rr0_v, rr1_v, ls_v, lr_v,
-    ho_v, hl_c, pl_c, e_v, t_v, a0_v, a1_v, acc_v, ps_v, pr_v,
+    ho_v, hs_v, hn_v, hl_c, pl_c, e_v, t_v, a0_v, a1_v, acc_v, ps_v, pr_v,
     in_sem, home_sem, w_sem, send_sem, recv_sem, rsend_sem, rrecv_sem,
 ):
     me = lax.axis_index("pool")
@@ -124,6 +112,11 @@
                 pltpu.make_async_copy(hv_h.at[part], hv_v.at[part], home_sem.at[1, c]),
             ]
         )
+    for c in range(home_chunks):
+        home[c][0].start()
+        home[c][1].start()
+    small[3].start()
+    small[4].start()
     order = [2, 1, 3, 0]
     weights = []
     for i, d in enumerate(order):
@@ -165,42 +158,59 @@
     for d in range(1, n):
         remote(0, tab_s.at[pool_peer(d)], tab_r.at[me], d).start()
     tab_r[me] = tab_s[me]
-    for c in range(home_chunks):
-        home[c][0].start()
-        home[c][1].start()
-    small[3].start()
-    small[4].start()
 
     for copy in small[:3]:
         copy.wait()
     sn_v[...] = nt(q_v[...].reshape(reqs * rows, HD), nk_v[...]).reshape(reqs, rows, HD)
+    t_row = iota(t_v.shape, 0)
+    t_col = iota(t_v.shape, 1)
+    t_v[...] = jnp.where(
+        t_row == (t_col // 128) * 16 + t_col % 16, 1.0, 0.0
+    ).astype(BF16)
     hl_c[...] = jnp.zeros(hl_c.shape, F32)
     pl_c[...] = jnp.zeros(pl_c.shape, F32)
     lane = iota((rows, 128), 1)
     row = iota((rows, 128), 0)
 
-    def home_request(r):
-        low = r * (2 * steps) + (row // (rows // 2)) * steps
-        seen = (lane >= low) & (lane <= low + row % steps)
-        new_scores = jnp.where(seen, sn_v[r], MASKED)
-        out, lse = attend(q_v[r], hk_v[r], hv_v[r], hlen[r], new_scores, nv_v[...])
-        ho_v[r] = out
-        return lse
-
-    def home_pair(i, carry):
-        lse0 = home_request(2 * i)
-        lse1 = home_request(2 * i + 1)
-        hl_c[0:rows] = jnp.where(
-            lane == 2 * i, lse0, jnp.where(lane == 2 * i + 1, lse1, hl_c[0:rows])
-        )
-        return carry
-
-    def home_part(c):
+    def home_part(c, between):
         home[c][0].wait()
+        total = hl_c[0:rows]
+        sums = []
+        for j in range(per_chunk):
+            r = c * per_chunk + j
+            low = r * (2 * steps) + (row // (rows // 2)) * steps
+            seen = (lane >= low) & (lane <= low + row % steps)
+            new_scores = jnp.where(seen, sn_v[r], MASKED)
+            scores = nt(wide_query(q_v[r]), hk_v[r])
+            scores = jnp.where(iota(scores.shape, 1) < hlen[r], scores, MASKED)
+            top = jnp.maximum(
+                jnp.max(scores, axis=1, keepdims=True),
+                jnp.max(new_scores, axis=1, keepdims=True),
+            )
+            shares = jnp.exp2((scores - top) * COEF)
+            new_shares = jnp.exp2((new_scores - top) * COEF)
+            summed = jnp.sum(shares, axis=1, keepdims=True) + jnp.sum(
+                new_shares, axis=1, keepdims=True
+            )
+            hs_v[j] = shares.astype(BF16)
+            hn_v[j] = new_shares.astype(BF16)
+            sums.append(summed)
+            total = jnp.where(lane == r, top * COEF + jnp.log2(summed), total)
+            between(j)
+        hl_c[0:rows] = total
         home[c][1].wait()
-        lax.fori_loop(c * per_chunk // 2, (c + 1) * per_chunk // 2, home_pair, 0)
-
-    home_part(0)
+        for j in range(per_chunk):
+            r = c * per_chunk + j
+            both = nn(hs_v[j], hv_v[r])
+            out = jnp.concatenate([both[:part_rows, :HD], both[part_rows:, HD:]], axis=0)
+            out = out + nn(hn_v[j], nv_v[...])
+            ho_v[r] = (out / sums[j]).astype(BF16)
+
+    def nothing(j):
+        pass
+
+    home_part(0, nothing)
+    home_part(1, nothing)
 
     all_of(0, tab_r).wait_recv()
 
@@ -220,12 +230,12 @@
     for copy in weights:
         copy.start()
 
-    home[1][0].wait()
-    home[1][1].wait()
-    for i in range(per_chunk // 2):
-        for d in range(1 + i * 16, min(n, 17 + i * 16)):
+    def query_sends(j):
+        for d in range(max(1, j * 8), j * 8 + 8):
             send_query(1, d)
-        home_pair(per_chunk // 2 + i, 0)
+
+    home_part(2, query_sends)
+    home_part(3, nothing)
     for d in range(n):
         inv_s[d] = inv_v[pool_peer(d), 0, 0]
 
@@ -268,12 +278,6 @@
                     if d > 0:
                         send_lse(d)
         rr[k][me] = res_v[inv_s[0], halves[k]]
-    for d in range(1, n):
-        send_result(1, d)
-
-    for c in range(2, home_chunks):
-        home_part(c)
-
     eight = iota((8, 128), 1) // 16 == iota((8, 128), 0)
     local = tab_r[...].reshape(n, 128)
     parts = n + reqs
@@ -292,12 +296,9 @@
     for i in range(16):
         same = (head_step == i // 4 * steps) & (owner_row == i % 4 * 4)
         e_v[i] = jnp.where(same, 1.0, 0.0).astype(BF16)
-    t_row = iota(t_v.shape, 0)
-    t_col = iota(t_v.shape, 1)
-    t_v[...] = jnp.where(
-        t_row == (t_col // 128) * 16 + t_col % 16, 1.0, 0.0
-    ).astype(BF16)
-
+        for d in (2 * i, 2 * i + 1):
+            if d > 0:
+                send_result(1, d)
     all_of(3, lr_v).wait_recv()
     lse = jnp.concatenate([lr_v[...].reshape(n, 128), hl_c[...].T[0:reqs]], axis=0)
     big = lse
@@ -464,6 +465,8 @@
             *[vmem((n, rows // 2, HD), BF16)] * 4,
             *[vmem((n, 1, 128), F32)] * 2,
             vmem((reqs, rows, HD), BF16),
+            vmem((reqs // chunks, rows, home_keys.shape[1]), BF16),
+            vmem((reqs // chunks, rows, 128), BF16),
             *[vmem((128, 128), F32)] * 2,
             vmem((16, 16, (n + reqs) * 16), BF16),
             vmem((128, (rows // 16) * 128), BF16),

time: 39.2 us -> 39.1 us (level)
  no operation moved by 1% of the time
where the time goes in v2:
time: 39.1 us; the launch traced here: 39 us
  Pallas kernels  38.4 us (98%)
  local copies, waits for them, and re-layouts  0.66 us (2%)
    pallas_call x1, Pallas kernels, per_device(): pl.pallas_call(functools.partial(kernel, n, t), out_shape=vmem((reqs // 2...  38.4 us

profile of v2, /device:TPU:0, one launch (start us, length us, event | category | flops | bytes accessed | tf_op | source)
XLA Modules:
  0.0 39.0 jit_solution(2485002692950744667)
XLA Ops:
  0.0 38.4 %lent_attention.1 = bf16[8,2,32,128]{3,2,1,0:T(8,128)(2,1)S(1)} custom-call(s32[16]{0:T(128)} %hlen_h.1, s32[16]{0:T(128)} %lreq_h.1, s32[16]{0:T(128)} %lblk_h.1, bf16[16,64,128]{2,1,0:T(8,128)(2,1)} %bitcast.21, bf16[128,128]{1,0:T(8,128)(2,1)} %bitcast.22, bf16[128,128]{1,0:T(8,128)(2,1)} %bitcast.23, bf16[16,512,256]{2,1,0:T(8,128)(2,1)} %hk_h.1, ...), custom_call_target="tpu_custom_call" | custom-call | tf_op jit(solution)/shard_map/lent_attention/pallas_call | solution.py:442
  38.4 0.7 %copy.17 = bf16[16,4,1024]{2,1,0:T(4,128)(2,1)} copy(bf16[16,4,1024]{2,1,0:T(4,128)(2,1)S(1)} %bitcast.20) | data formatting | bytes 262144

commit v3 on v2

--- a/solution.py
+++ b/solution.py
@@ -17,6 +17,14 @@
 F32 = jnp.float32
 BF16 = jnp.bfloat16
 COEF = math.log2(math.e) / math.sqrt(HD)
+
+
+def hops(d):
+    dy, dx = d // 8, d // 2 % 4
+    return min(dy, 4 - dy) + min(dx, 4 - dx)
+
+
+FAR_FIRST = sorted(range(1, 32), key=lambda d: -hops(d))
 
 
 def nt(a, b):
@@ -83,13 +91,13 @@
 
     barrier = pltpu.get_barrier_semaphore()
 
-    for d in range(1, n):
-        pl.semaphore_signal(
-            barrier, inc=1, device_id={"pool": pool_peer(d)}, device_id_type=MESH
-        )
     for d in range(1, t):
         pl.semaphore_signal(
             barrier, inc=1, device_id={"tp": tp_peer(d)}, device_id_type=MESH
+        )
+    for d in FAR_FIRST:
+        pl.semaphore_signal(
+            barrier, inc=1, device_id={"pool": pool_peer(d)}, device_id_type=MESH
         )
 
     small = [
@@ -155,7 +163,7 @@
 
     pl.semaphore_wait(barrier, n - 1 + t - 1)
 
-    for d in range(1, n):
+    for d in FAR_FIRST:
         remote(0, tab_s.at[pool_peer(d)], tab_r.at[me], d).start()
     tab_r[me] = tab_s[me]
 
@@ -214,24 +222,24 @@
 
     all_of(0, tab_r).wait_recv()
 
-    picks = [jnp.maximum(tab_r[pool_peer(d), 0, 0], 0) for d in range(1, n)]
+    picks = {d: jnp.maximum(tab_r[pool_peer(d), 0, 0], 0) for d in FAR_FIRST}
     mine = jnp.maximum(tab_r[me, 0, 0], 0)
     halves = [slice(0, part_rows), slice(part_rows, rows)]
 
     def send_query(k, d):
         peer = pool_peer(d)
-        qs[k][peer] = q_v[picks[d - 1], halves[k]]
+        qs[k][peer] = q_v[picks[d], halves[k]]
         remote(1 + k, qs[k].at[peer], qr[k].at[me], d).start()
 
     for k in range(2):
         qr[k][me] = q_v[mine, halves[k]]
-    for d in range(1, n):
+    for d in FAR_FIRST:
         send_query(0, d)
     for copy in weights:
         copy.start()
 
     def query_sends(j):
-        for d in range(max(1, j * 8), j * 8 + 8):
+        for d in FAR_FIRST[j * 8 : j * 8 + 8]:
             send_query(1, d)
 
     home_part(2, query_sends)
@@ -263,9 +271,8 @@
             sums.append(summed)
             total = jnp.where(part_lane == owner, lse, total)
             if k == 1:
-                for d in (2 * l, 2 * l + 1):
-                    if d > 0:
-                        send_result(0, d)
+                for d in FAR_FIRST[2 * l : 2 * l + 2]:
+                    send_result(0, d)
         pl_c[halves[k]] = total
         if k == 1:
             ls_v[...] = pl_c[...].T[0:n].reshape(n, 1, 128)
@@ -274,9 +281,8 @@
             out = nn(sh_v[l], pv_v[l, :, width])
             res_v[l, halves[k]] = (out / sums[l]).astype(BF16)
             if k == 1:
-                for d in (2 * l, 2 * l + 1):
-                    if d > 0:
-                        send_lse(d)
+                for d in FAR_FIRST[2 * l : 2 * l + 2]:
+                    send_lse(d)
         rr[k][me] = res_v[inv_s[0], halves[k]]
     eight = iota((8, 128), 1) // 16 == iota((8, 128), 0)
     local = tab_r[...].reshape(n, 128)
@@ -296,9 +302,8 @@
     for i in range(16):
         same = (head_step == i // 4 * steps) & (owner_row == i % 4 * 4)
         e_v[i] = jnp.where(same, 1.0, 0.0).astype(BF16)
-        for d in (2 * i, 2 * i + 1):
-            if d > 0:
-                send_result(1, d)
+        for d in FAR_FIRST[2 * i : 2 * i + 2]:
+            send_result(1, d)
     all_of(3, lr_v).wait_recv()
     lse = jnp.concatenate([lr_v[...].reshape(n, 128), hl_c[...].T[0:reqs]], axis=0)
     big = lse
@@ -350,10 +355,11 @@
         acc_v[i] = nn(a0_v[...], w_v[i, 0:deep])
     merge(1, a1_v)
 
-    def projected(i):
-        return acc_v[i] + nn(a1_v[...], w_v[i, deep : 2 * deep])
-
     half = cols // 2
+    left, right = slice(0, half), slice(half, cols)
+
+    def projected(i, at):
+        return acc_v[i, :, at] + nn(a1_v[...], w_v[i, deep : 2 * deep, at])
 
     def to_neighbour(i, src, side):
         return pltpu.make_async_remote_copy(
@@ -366,34 +372,30 @@
         )
 
     up, down = 1, t - 1
-    hops = [
+    ring = [
         to_neighbour(i, ps_v.at[i], side)
         for i, side in enumerate([up, down, up, down, up, down])
     ]
-    for i in range(2):
-        at = slice(i * half, i * half + half)
-        value = acc_v[0, :, at] + nn(a1_v[...], w_v[0, deep : 2 * deep, at])
+    def send(i, value):
         ps_v[i] = value.astype(BF16)
-        hops[i].start()
-    above = projected(1)
-    ps_v[2] = above[:, half:].astype(BF16)
-    hops[2].start()
-    acc_v[1, :, :half] = above[:, :half]
-    below = projected(2)
-    ps_v[3] = below[:, :half].astype(BF16)
-    hops[3].start()
-    hops[0].wait_recv()
-    ps_v[4] = (acc_v[1, :, :half] + pr_v[0].astype(F32)).astype(BF16)
-    hops[4].start()
-    hops[1].wait_recv()
-    ps_v[5] = (below[:, half:] + pr_v[1].astype(F32)).astype(BF16)
-    hops[5].start()
-    acc_v[3] = projected(3)
+        ring[i].start()
+
+    send(0, projected(0, left))
+    send(1, projected(0, right))
+    send(2, projected(1, right))
+    send(3, projected(2, left))
+    above = projected(1, left)
+    ring[0].wait_recv()
+    send(4, above + pr_v[0].astype(F32))
+    below = projected(2, right)
+    ring[1].wait_recv()
+    send(5, below + pr_v[1].astype(F32))
+    own = jnp.concatenate([projected(3, left), projected(3, right)], axis=1)
     for i in range(2, 6):
-        hops[i].wait_recv()
+        ring[i].wait_recv()
     from_below = jnp.concatenate([pr_v[4], pr_v[2]], axis=1).astype(F32)
     from_above = jnp.concatenate([pr_v[3], pr_v[5]], axis=1).astype(F32)
-    result = acc_v[3] + from_below + from_above
+    result = own + from_below + from_above
 
     first = iota((8, 8, HD), 1) < 4
     for g in range(2):
@@ -412,8 +414,8 @@
         all_of(1 + k, qs[k]).wait_send()
         all_of(4 + k, rs[k]).wait_send()
     all_of(3, ls_v).wait_send()
-    for hop in hops:
-        hop.wait_send()
+    for copy in ring:
+        copy.wait_send()
 
 
 def per_device(

time: 39.1 us -> 38.8 us (level)
  Pallas kernels: 38.4 us -> 38 us
where the time goes in v3:
time: 38.8 us; the launch traced here: 38.7 us
  Pallas kernels  38 us (98%)
  local copies, waits for them, and re-layouts  0.66 us (2%)
    pallas_call x1, Pallas kernels, per_device(): pl.pallas_call(functools.partial(kernel, n, t), out_shape=vmem((reqs // 2...  38 us

profile of v3, /device:TPU:0, one launch (start us, length us, event | category | flops | bytes accessed | tf_op | source)
XLA Modules:
  0.0 38.7 jit_solution(9406230133191006812)
XLA Ops:
  0.0 38.0 %lent_attention.1 = bf16[8,2,32,128]{3,2,1,0:T(8,128)(2,1)S(1)} custom-call(s32[16]{0:T(128)} %hlen_h.1, s32[16]{0:T(128)} %lreq_h.1, s32[16]{0:T(128)} %lblk_h.1, bf16[16,64,128]{2,1,0:T(8,128)(2,1)} %bitcast.21, bf16[128,128]{1,0:T(8,128)(2,1)} %bitcast.22, bf16[128,128]{1,0:T(8,128)(2,1)} %bitcast.23, bf16[16,512,256]{2,1,0:T(8,128)(2,1)} %hk_h.1, ...), custom_call_target="tpu_custom_call" | custom-call | tf_op jit(solution)/shard_map/lent_attention/pallas_call | solution.py:444
  38.0 0.7 %copy.17 = bf16[16,4,1024]{2,1,0:T(4,128)(2,1)} copy(bf16[16,4,1024]{2,1,0:T(4,128)(2,1)S(1)} %bitcast.20) | data formatting | bytes 262144

commit v4 on v3

--- a/solution.py
+++ b/solution.py
@@ -67,7 +67,7 @@
     hlen, lreq, lblk, q_v, nk_v, nv_v, hk_v, hv_v, pk_v, pv_v, w_v,
     sn_v, tab_s, tab_r, inv_v, inv_s,
     qs0_v, qs1_v, qr0_v, qr1_v, res_v, sh_v, rs0_v, rs1_v, rr0_v, rr1_v, ls_v, lr_v,
-    ho_v, hs_v, hn_v, hl_c, pl_c, e_v, t_v, a0_v, a1_v, acc_v, ps_v, pr_v,
+    ho_v, hs_v, hn_v, hl_c, pl_c, e_v, t_v, l_v, a0_v, a1_v, acc_v, ps_v, pr_v,
     in_sem, home_sem, w_sem, send_sem, recv_sem, rsend_sem, rrecv_sem,
 ):
     me = lax.axis_index("pool")
@@ -270,9 +270,6 @@
             sh_v[l] = shares
             sums.append(summed)
             total = jnp.where(part_lane == owner, lse, total)
-            if k == 1:
-                for d in FAR_FIRST[2 * l : 2 * l + 2]:
-                    send_result(0, d)
         pl_c[halves[k]] = total
         if k == 1:
             ls_v[...] = pl_c[...].T[0:n].reshape(n, 1, 128)
@@ -284,6 +281,9 @@
                 for d in FAR_FIRST[2 * l : 2 * l + 2]:
                     send_lse(d)
         rr[k][me] = res_v[inv_s[0], halves[k]]
+        if k == 0:
+            for d in FAR_FIRST:
+                send_result(0, d)
     eight = iota((8, 128), 1) // 16 == iota((8, 128), 0)
     local = tab_r[...].reshape(n, 128)
     parts = n + reqs
@@ -319,41 +319,43 @@
         )
     spread = nn((share / total).astype(BF16), t_v[...])
 
-    def merge(k, a_v):
+    def build(g):
+        wide = g * 128
+        along = jnp.concatenate(
+            [
+                jnp.sum(
+                    jnp.where(eight, spread[c * 8 : c * 8 + 8, wide : wide + 128], 0.0),
+                    axis=0,
+                    keepdims=True,
+                )
+                for c in range(parts // 8)
+            ],
+            axis=1,
+        )
+        along = jnp.broadcast_to(along, block).astype(BF16)
+        return (e_v[...] * along[None]).reshape(256, parts * 16)
+
+    def merge(k, a_v, lefts):
         all_of(4 + k, rr[k]).wait_recv()
         for g in range(part_rows // 16):
-            wide = (k * (part_rows // 16) + g) * 128
-            along = jnp.concatenate(
-                [
-                    jnp.sum(
-                        jnp.where(
-                            eight, spread[c * 8 : c * 8 + 8, wide : wide + 128], 0.0
-                        ),
-                        axis=0,
-                        keepdims=True,
-                    )
-                    for c in range(parts // 8)
-                ],
-                axis=1,
-            )
-            along = jnp.broadcast_to(along, block).astype(BF16)
-            left = (e_v[...] * along[None]).reshape(256, parts * 16)
             group = slice(g * 16, g * 16 + 16)
             own = slice(k * part_rows + g * 16, k * part_rows + g * 16 + 16)
             right = jnp.concatenate(
                 [rr[k][:, group].reshape(n * 16, HD), ho_v[:, own].reshape(reqs * 16, HD)],
                 axis=0,
             )
-            merged = nn(left, right).astype(BF16)
+            merged = nn(lefts(g), right).astype(BF16)
             for h in range(4):
                 head = g * 4 + h
                 a_v[:, head * HD : head * HD + HD] = merged[h * rows : h * rows + rows]
 
-    merge(0, a0_v)
+    for g in range(2):
+        l_v[g] = build(2 + g)
+    merge(0, a0_v, build)
     for i in range(t):
         weights[i].wait()
         acc_v[i] = nn(a0_v[...], w_v[i, 0:deep])
-    merge(1, a1_v)
+    merge(1, a1_v, lambda g: l_v[g])
 
     half = cols // 2
     left, right = slice(0, half), slice(half, cols)
@@ -472,6 +474,7 @@
             *[vmem((128, 128), F32)] * 2,
             vmem((16, 16, (n + reqs) * 16), BF16),
             vmem((128, (rows // 16) * 128), BF16),
+            vmem((2, 256, (n + reqs) * 16), BF16),
             *[vmem((reqs * steps, features // 2), BF16)] * 2,
             vmem((t, reqs * steps, cols), F32),
             vmem((6, reqs * steps, cols // 2), BF16),

time: 38.8 us -> 38.5 us (level)
  no operation moved by 1% of the time
where the time goes in v4:
time: 38.5 us; the launch traced here: 38.4 us
  Pallas kernels  37.8 us (98%)
  local copies, waits for them, and re-layouts  0.66 us (2%)
    pallas_call x1, Pallas kernels, per_device(): pl.pallas_call(functools.partial(kernel, n, t), out_shape=vmem((reqs // 2...  37.8 us

profile of v4, /device:TPU:0, one launch (start us, length us, event | category | flops | bytes accessed | tf_op | source)
XLA Modules:
  0.0 38.4 jit_solution(18273711000581576659)
XLA Ops:
  0.0 37.8 %lent_attention.1 = bf16[8,2,32,128]{3,2,1,0:T(8,128)(2,1)S(1)} custom-call(s32[16]{0:T(128)} %hlen_h.1, s32[16]{0:T(128)} %lreq_h.1, s32[16]{0:T(128)} %lblk_h.1, bf16[16,64,128]{2,1,0:T(8,128)(2,1)} %bitcast.21, bf16[128,128]{1,0:T(8,128)(2,1)} %bitcast.22, bf16[128,128]{1,0:T(8,128)(2,1)} %bitcast.23, bf16[16,512,256]{2,1,0:T(8,128)(2,1)} %hk_h.1, ...), custom_call_target="tpu_custom_call" | custom-call | tf_op jit(solution)/shard_map/lent_attention/pallas_call | solution.py:446
  37.8 0.7 %copy.17 = bf16[16,4,1024]{2,1,0:T(4,128)(2,1)} copy(bf16[16,4,1024]{2,1,0:T(4,128)(2,1)S(1)} %bitcast.20) | data formatting | bytes 262144

commit v5 on v4

--- a/solution.py
+++ b/solution.py
@@ -166,15 +166,12 @@
     for d in FAR_FIRST:
         remote(0, tab_s.at[pool_peer(d)], tab_r.at[me], d).start()
     tab_r[me] = tab_s[me]
+    for copy in weights:
+        copy.start()
 
     for copy in small[:3]:
         copy.wait()
     sn_v[...] = nt(q_v[...].reshape(reqs * rows, HD), nk_v[...]).reshape(reqs, rows, HD)
-    t_row = iota(t_v.shape, 0)
-    t_col = iota(t_v.shape, 1)
-    t_v[...] = jnp.where(
-        t_row == (t_col // 128) * 16 + t_col % 16, 1.0, 0.0
-    ).astype(BF16)
     hl_c[...] = jnp.zeros(hl_c.shape, F32)
     pl_c[...] = jnp.zeros(pl_c.shape, F32)
     lane = iota((rows, 128), 1)
@@ -218,7 +215,6 @@
         pass
 
     home_part(0, nothing)
-    home_part(1, nothing)
 
     all_of(0, tab_r).wait_recv()
 
@@ -235,15 +231,19 @@
         qr[k][me] = q_v[mine, halves[k]]
     for d in FAR_FIRST:
         send_query(0, d)
-    for copy in weights:
-        copy.start()
 
     def query_sends(j):
         for d in FAR_FIRST[j * 8 : j * 8 + 8]:
             send_query(1, d)
 
-    home_part(2, query_sends)
+    home_part(1, query_sends)
+    home_part(2, nothing)
     home_part(3, nothing)
+    t_row = iota(t_v.shape, 0)
+    t_col = iota(t_v.shape, 1)
+    t_v[...] = jnp.where(
+        t_row == (t_col // 128) * 16 + t_col % 16, 1.0, 0.0
+    ).astype(BF16)
     for d in range(n):
         inv_s[d] = inv_v[pool_peer(d), 0, 0]
 

time: 38.5 us -> 38.5 us (level)
  no operation moved by 1% of the time
where the time goes in v5:
time: 38.5 us; the launch traced here: 38.4 us
  Pallas kernels  37.8 us (98%)
  local copies, waits for them, and re-layouts  0.66 us (2%)
    pallas_call x1, Pallas kernels, per_device(): pl.pallas_call(functools.partial(kernel, n, t), out_shape=vmem((reqs // 2...  37.8 us

profile of v5, /device:TPU:0, one launch (start us, length us, event | category | flops | bytes accessed | tf_op | source)
XLA Modules:
  0.0 38.4 jit_solution(18089278728116725908)
XLA Ops:
  0.0 37.8 %lent_attention.1 = bf16[8,2,32,128]{3,2,1,0:T(8,128)(2,1)S(1)} custom-call(s32[16]{0:T(128)} %hlen_h.1, s32[16]{0:T(128)} %lreq_h.1, s32[16]{0:T(128)} %lblk_h.1, bf16[16,64,128]{2,1,0:T(8,128)(2,1)} %bitcast.21, bf16[128,128]{1,0:T(8,128)(2,1)} %bitcast.22, bf16[128,128]{1,0:T(8,128)(2,1)} %bitcast.23, bf16[16,512,256]{2,1,0:T(8,128)(2,1)} %hk_h.1, ...), custom_call_target="tpu_custom_call" | custom-call | tf_op jit(solution)/shard_map/lent_attention/pallas_call | solution.py:446
  37.8 0.7 %copy.17 = bf16[16,4,1024]{2,1,0:T(4,128)(2,1)} copy(bf16[16,4,1024]{2,1,0:T(4,128)(2,1)S(1)} %bitcast.20) | data formatting | bytes 262144

commit v6 on v4

--- a/solution.py
+++ b/solution.py
@@ -83,8 +83,10 @@
     qs, qr = (qs0_v, qs1_v), (qr0_v, qr1_v)
     rs, rr = (rs0_v, rs1_v), (rr0_v, rr1_v)
 
+    peers = {d: jnp.where(me + d >= n, me + d - n, me + d) for d in range(n)}
+
     def pool_peer(d):
-        return jnp.where(me + d >= n, me + d - n, me + d)
+        return peers[d]
 
     def tp_peer(d):
         return lax.rem(tp + d, t)
@@ -93,11 +95,11 @@
 
     for d in range(1, t):
         pl.semaphore_signal(
-            barrier, inc=1, device_id={"tp": tp_peer(d)}, device_id_type=MESH
+            barrier, inc=1, device_id={"tp": tp_peer(d), "pool": me}, device_id_type=MESH
         )
     for d in FAR_FIRST:
         pl.semaphore_signal(
-            barrier, inc=1, device_id={"pool": pool_peer(d)}, device_id_type=MESH
+            barrier, inc=1, device_id={"tp": tp, "pool": pool_peer(d)}, device_id_type=MESH
         )
 
     small = [
@@ -153,7 +155,7 @@
             dst_ref=dst,
             send_sem=send_sem.at[phase],
             recv_sem=recv_sem.at[phase],
-            device_id={"pool": pool_peer(d)},
+            device_id={"tp": tp, "pool": pool_peer(d)},
             device_id_type=MESH,
         )
 
@@ -369,7 +371,7 @@
             dst_ref=pr_v.at[i],
             send_sem=rsend_sem.at[i],
             recv_sem=rrecv_sem.at[i],
-            device_id={"tp": tp_peer(side)},
+            device_id={"tp": tp_peer(side), "pool": me},
             device_id_type=MESH,
         )
 

time: 38.5 us -> 38.5 us (level)
  no operation moved by 1% of the time
where the time goes in v6:
time: 38.5 us; the launch traced here: 38.4 us
  Pallas kernels  37.8 us (98%)
  local copies, waits for them, and re-layouts  0.66 us (2%)
    pallas_call x1, Pallas kernels, per_device(): pl.pallas_call(functools.partial(kernel, n, t), out_shape=vmem((reqs // 2...  37.8 us

profile of v6, /device:TPU:0, one launch (start us, length us, event | category | flops | bytes accessed | tf_op | source)
XLA Modules:
  0.0 38.4 jit_solution(7376700024121766131)
XLA Ops:
  0.0 37.8 %lent_attention.1 = bf16[8,2,32,128]{3,2,1,0:T(8,128)(2,1)S(1)} custom-call(s32[16]{0:T(128)} %hlen_h.1, s32[16]{0:T(128)} %lreq_h.1, s32[16]{0:T(128)} %lblk_h.1, bf16[16,64,128]{2,1,0:T(8,128)(2,1)} %bitcast.21, bf16[128,128]{1,0:T(8,128)(2,1)} %bitcast.22, bf16[128,128]{1,0:T(8,128)(2,1)} %bitcast.23, bf16[16,512,256]{2,1,0:T(8,128)(2,1)} %hk_h.1, ...), custom_call_target="tpu_custom_call" | custom-call | tf_op jit(solution)/shard_map/lent_attention/pallas_call | solution.py:448
  37.8 0.7 %copy.17 = bf16[16,4,1024]{2,1,0:T(4,128)(2,1)} copy(bf16[16,4,1024]{2,1,0:T(4,128)(2,1)S(1)} %bitcast.20) | data formatting | bytes 262144

commit v7 on v6

--- a/solution.py
+++ b/solution.py
@@ -19,12 +19,7 @@
 COEF = math.log2(math.e) / math.sqrt(HD)
 
 
-def hops(d):
-    dy, dx = d // 8, d // 2 % 4
-    return min(dy, 4 - dy) + min(dx, 4 - dx)
-
-
-FAR_FIRST = sorted(range(1, 32), key=lambda d: -hops(d))
+ORDER = list(range(1, 32))
 
 
 def nt(a, b):
@@ -83,7 +78,14 @@
     qs, qr = (qs0_v, qs1_v), (qr0_v, qr1_v)
     rs, rr = (rs0_v, rs1_v), (rr0_v, rr1_v)
 
-    peers = {d: jnp.where(me + d >= n, me + d - n, me + d) for d in range(n)}
+    core = lax.rem(me, 2)
+    turn = 1 - 2 * core
+    ys = [lax.rem(me // 8 + turn * d + 4, 4) for d in range(4)]
+    xs = [lax.rem(me // 2 % 4 + turn * d + 4, 4) for d in range(4)]
+    peers = {
+        k: (ys[k % 4] * 4 + xs[(k // 4 + k) % 4]) * 2 + (core if k < 16 else 1 - core)
+        for k in range(n)
+    }
 
     def pool_peer(d):
         return peers[d]
@@ -97,7 +99,7 @@
         pl.semaphore_signal(
             barrier, inc=1, device_id={"tp": tp_peer(d), "pool": me}, device_id_type=MESH
         )
-    for d in FAR_FIRST:
+    for d in ORDER:
         pl.semaphore_signal(
             barrier, inc=1, device_id={"tp": tp, "pool": pool_peer(d)}, device_id_type=MESH
         )
@@ -165,7 +167,7 @@
 
     pl.semaphore_wait(barrier, n - 1 + t - 1)
 
-    for d in FAR_FIRST:
+    for d in ORDER:
         remote(0, tab_s.at[pool_peer(d)], tab_r.at[me], d).start()
     tab_r[me] = tab_s[me]
 
@@ -224,7 +226,7 @@
 
     all_of(0, tab_r).wait_recv()
 
-    picks = {d: jnp.maximum(tab_r[pool_peer(d), 0, 0], 0) for d in FAR_FIRST}
+    picks = {d: jnp.maximum(tab_r[pool_peer(d), 0, 0], 0) for d in ORDER}
     mine = jnp.maximum(tab_r[me, 0, 0], 0)
     halves = [slice(0, part_rows), slice(part_rows, rows)]
 
@@ -235,13 +237,13 @@
 
     for k in range(2):
         qr[k][me] = q_v[mine, halves[k]]
-    for d in FAR_FIRST:
+    for d in ORDER:
         send_query(0, d)
     for copy in weights:
         copy.start()
 
     def query_sends(j):
-        for d in FAR_FIRST[j * 8 : j * 8 + 8]:
+        for d in ORDER[j * 8 : j * 8 + 8]:
             send_query(1, d)
 
     home_part(2, query_sends)
@@ -280,11 +282,11 @@
             out = nn(sh_v[l], pv_v[l, :, width])
             res_v[l, halves[k]] = (out / sums[l]).astype(BF16)
             if k == 1:
-                for d in FAR_FIRST[2 * l : 2 * l + 2]:
+                for d in ORDER[2 * l : 2 * l + 2]:
                     send_lse(d)
         rr[k][me] = res_v[inv_s[0], halves[k]]
         if k == 0:
-            for d in FAR_FIRST:
+            for d in ORDER:
                 send_result(0, d)
     eight = iota((8, 128), 1) // 16 == iota((8, 128), 0)
     local = tab_r[...].reshape(n, 128)
@@ -304,7 +306,7 @@
     for i in range(16):
         same = (head_step == i // 4 * steps) & (owner_row == i % 4 * 4)
         e_v[i] = jnp.where(same, 1.0, 0.0).astype(BF16)
-        for d in FAR_FIRST[2 * i : 2 * i + 2]:
+        for d in ORDER[2 * i : 2 * i + 2]:
             send_result(1, d)
     all_of(3, lr_v).wait_recv()
     lse = jnp.concatenate([lr_v[...].reshape(n, 128), hl_c[...].T[0:reqs]], axis=0)

time: 38.5 us -> 38.7 us (level)
  no operation moved by 1% of the time
where the time goes in v7:
time: 38.7 us; the launch traced here: 38.6 us
  Pallas kernels  37.9 us (98%)
  local copies, waits for them, and re-layouts  0.66 us (2%)
    pallas_call x1, Pallas kernels, per_device(): pl.pallas_call(functools.partial(kernel, n, t), out_shape=vmem((reqs // 2...  37.9 us

profile of v7, /device:TPU:0, one launch (start us, length us, event | category | flops | bytes accessed | tf_op | source)
XLA Modules:
  0.0 38.6 jit_solution(5209499442505543762)
XLA Ops:
  0.0 37.9 %lent_attention.1 = bf16[8,2,32,128]{3,2,1,0:T(8,128)(2,1)S(1)} custom-call(s32[16]{0:T(128)} %hlen_h.1, s32[16]{0:T(128)} %lreq_h.1, s32[16]{0:T(128)} %lblk_h.1, bf16[16,64,128]{2,1,0:T(8,128)(2,1)} %bitcast.21, bf16[128,128]{1,0:T(8,128)(2,1)} %bitcast.22, bf16[128,128]{1,0:T(8,128)(2,1)} %bitcast.23, bf16[16,512,256]{2,1,0:T(8,128)(2,1)} %hk_h.1, ...), custom_call_target="tpu_custom_call" | custom-call | tf_op jit(solution)/shard_map/lent_attention/pallas_call | solution.py:450
  37.9 0.7 %copy.17 = bf16[16,4,1024]{2,1,0:T(4,128)(2,1)} copy(bf16[16,4,1024]{2,1,0:T(4,128)(2,1)S(1)} %bitcast.20) | data formatting | bytes 262144

commit v8 on v6

--- a/solution.py
+++ b/solution.py
@@ -66,7 +66,7 @@
     out_ref,
     hlen, lreq, lblk, q_v, nk_v, nv_v, hk_v, hv_v, pk_v, pv_v, w_v,
     sn_v, tab_s, tab_r, inv_v, inv_s,
-    qs0_v, qs1_v, qr0_v, qr1_v, res_v, sh_v, rs0_v, rs1_v, rr0_v, rr1_v, ls_v, lr_v,
+    qs_v, qr_v, res_v, sh_v, rs0_v, rs1_v, rr0_v, rr1_v, ls_v, lr_v,
     ho_v, hs_v, hn_v, hl_c, pl_c, e_v, t_v, l_v, a0_v, a1_v, acc_v, ps_v, pr_v,
     in_sem, home_sem, w_sem, send_sem, recv_sem, rsend_sem, rrecv_sem,
 ):
@@ -80,7 +80,6 @@
     cols = w_v.shape[2]
     part_rows = rows // 2
     deep = a0_v.shape[1]
-    qs, qr = (qs0_v, qs1_v), (qr0_v, qr1_v)
     rs, rr = (rs0_v, rs1_v), (rr0_v, rr1_v)
 
     peers = {d: jnp.where(me + d >= n, me + d - n, me + d) for d in range(n)}
@@ -228,23 +227,18 @@
     mine = jnp.maximum(tab_r[me, 0, 0], 0)
     halves = [slice(0, part_rows), slice(part_rows, rows)]
 
-    def send_query(k, d):
+    def send_query(d):
         peer = pool_peer(d)
-        qs[k][peer] = q_v[picks[d], halves[k]]
-        remote(1 + k, qs[k].at[peer], qr[k].at[me], d).start()
-
-    for k in range(2):
-        qr[k][me] = q_v[mine, halves[k]]
+        qs_v[peer] = q_v[picks[d]]
+        remote(1, qs_v.at[peer], qr_v.at[me], d).start()
+
+    qr_v[me] = q_v[mine]
     for d in FAR_FIRST:
-        send_query(0, d)
+        send_query(d)
     for copy in weights:
         copy.start()
 
-    def query_sends(j):
-        for d in FAR_FIRST[j * 8 : j * 8 + 8]:
-            send_query(1, d)
-
-    home_part(2, query_sends)
+    home_part(2, nothing)
     home_part(3, nothing)
     for d in range(n):
         inv_s[d] = inv_v[pool_peer(d), 0, 0]
@@ -261,17 +255,20 @@
     def send_lse(d):
         remote(3, ls_v.at[pool_peer(d)], lr_v.at[me], d).start()
 
+    all_of(1, qr_v).wait_recv()
     for k in range(2):
-        all_of(1 + k, qr[k]).wait_recv()
         width = slice(k * HD, k * HD + HD)
         total = jnp.zeros((part_rows, 128), F32)
         sums = []
         for l in range(slots):
             owner = lreq[l] // reqs
-            shares, summed, lse = head_shares(qr[k][owner], pk_v[l, :, width], lblk[l] * BLOCK)
+            shares, summed, lse = head_shares(qr_v[owner, halves[k]], pk_v[l, :, width], lblk[l] * BLOCK)
             sh_v[l] = shares
             sums.append(summed)
             total = jnp.where(part_lane == owner, lse, total)
+            if k == 1:
+                for d in FAR_FIRST[2 * l : 2 * l + 2]:
+                    send_result(0, d)
         pl_c[halves[k]] = total
         if k == 1:
             ls_v[...] = pl_c[...].T[0:n].reshape(n, 1, 128)
@@ -283,9 +280,6 @@
                 for d in FAR_FIRST[2 * l : 2 * l + 2]:
                     send_lse(d)
         rr[k][me] = res_v[inv_s[0], halves[k]]
-        if k == 0:
-            for d in FAR_FIRST:
-                send_result(0, d)
     eight = iota((8, 128), 1) // 16 == iota((8, 128), 0)
     local = tab_r[...].reshape(n, 128)
     parts = n + reqs
@@ -415,8 +409,8 @@
 
     all_of(0, tab_s).wait_send()
     for k in range(2):
-        all_of(1 + k, qs[k]).wait_send()
         all_of(4 + k, rs[k]).wait_send()
+    all_of(1, qs_v).wait_send()
     all_of(3, ls_v).wait_send()
     for copy in ring:
         copy.wait_send()
@@ -465,7 +459,7 @@
             vmem((n, 1, 128), jnp.int32),
             vmem((n, 1, 128), jnp.int32),
             pltpu.SMEM((n,), jnp.int32),
-            *[vmem((n, rows // 2, HD), BF16)] * 4,
+            *[vmem((n, rows, HD), BF16)] * 2,
             vmem((slots, rows, HD), BF16),
             vmem((slots, rows // 2, piece), BF16),
             *[vmem((n, rows // 2, HD), BF16)] * 4,

time: 38.5 us -> 39.2 us (1.018)
  Pallas kernels: 37.8 us -> 38.4 us
    pallas_call x1, Pallas kernels: 37.8 us -> 38.4 us  [per_device(): pl.pallas_call(functools.partial(kernel, n, t), out_shape=vmem((reqs // 2...]
where the time goes in v8:
time: 39.2 us; the launch traced here: 39.1 us
  Pallas kernels  38.4 us (98%)
  local copies, waits for them, and re-layouts  0.66 us (2%)
    pallas_call x1, Pallas kernels, per_device(): pl.pallas_call(functools.partial(kernel, n, t), out_shape=vmem((reqs // 2...  38.4 us

profile of v8, /device:TPU:0, one launch (start us, length us, event | category | flops | bytes accessed | tf_op | source)
XLA Modules:
  0.0 39.1 jit_solution(1258958982922420501)
XLA Ops:
  0.0 38.4 %lent_attention.1 = bf16[8,2,32,128]{3,2,1,0:T(8,128)(2,1)S(1)} custom-call(s32[16]{0:T(128)} %hlen_h.1, s32[16]{0:T(128)} %lreq_h.1, s32[16]{0:T(128)} %lblk_h.1, bf16[16,64,128]{2,1,0:T(8,128)(2,1)} %bitcast.21, bf16[128,128]{1,0:T(8,128)(2,1)} %bitcast.22, bf16[128,128]{1,0:T(8,128)(2,1)} %bitcast.23, bf16[16,512,256]{2,1,0:T(8,128)(2,1)} %hk_h.1, ...), custom_call_target="tpu_custom_call" | custom-call | tf_op jit(solution)/shard_map/lent_attention/pallas_call | solution.py:442
  38.4 0.7 %copy.17 = bf16[16,4,1024]{2,1,0:T(4,128)(2,1)} copy(bf16[16,4,1024]{2,1,0:T(4,128)(2,1)S(1)} %bitcast.20) | data formatting | bytes 262144
